TPU v7x, 128 devices: a whole 4x4x4 slice. The times are simulated.
128 devices in a mesh: row: 8 (over y, core), col: 16 (over x, z).
Axes of the slice: x: 4, y: 4, z: 4, core: 2. Of those that a mesh axis runs over, the one named last changes fastest.
Arguments:
- blk_u: bfloat16 [96, 128, 64, 512], P('row', 'col'), may hold values from -6 to 6
- blk_v: bfloat16 [96, 128, 64, 512], P('row', 'col'), may hold values from -0.75 to 0.75
- prow_u: bfloat16 [96, 64, 512], P('col'), may hold values from -6 to 6
- prow_v: bfloat16 [96, 64, 512], P('col'), may hold values from -0.1875 to 0.1875
- pcol_u: bfloat16 [128, 64, 512], P('row'), may hold values from -6 to 6
- pcol_v: bfloat16 [128, 64, 512], P('row'), may hold values from -0.1875 to 0.1875
- linv: bfloat16 [512, 512], P('col'), may hold values from -0.15 to 1.4, as said below
- omega: bfloat16 [64, 512], replicated, may hold values from -0.25 to 0.25
- child_u: bfloat16 [2048, 64, 512], P(('row', 'col')), may hold values from -6 to 6
- child_v: bfloat16 [2048, 64, 512], P(('row', 'col')), may hold values from -0.75 to 0.75
- child_dest: int32 [2048, 1], P(('row', 'col')), may hold values from 0 to 15; in each aligned block of 16 rows (0 to 15, 16 to 31, ...) at most 2 rows name the same one
- child_block: int32 [2048], P(('row', 'col')), may hold values from 0 to 95
Outputs:
- sketch: bfloat16 [96, 128, 64, 512], P('row', 'col')
- prow_l: bfloat16 [96, 64, 512], P('col')
- pcol_l: bfloat16 [128, 64, 512], P('row')
Inputs may be any that keep to these rules, and one draw needn't show every extreme that they name: `linv`: lower triangular with diagonal entries of about 0.6 to 1.4. `child_dest`: in the 16 child blocks of one device at most 2 name the same column index, and some column index is named 2 times.
All inputs are finite; a program needn't handle non-finite values.
Results may differ from a plain program's by a relative error of at most 0.0065.
Values may be sent and summed in bfloat16 or wider, within the bound.
A program may use at most 192 MiB of HBM per device.

v0:
```python
import jax
import jax.numpy as jnp
from jax import lax
from jax.sharding import PartitionSpec as P

CAP = 2


def body(
    blk_u,
    blk_v,
    prow_u,
    prow_v,
    pcol_u,
    pcol_v,
    linv,
    omega,
    child_u,
    child_v,
    child_dest,
    child_block,
):
    fl = jnp.float32
    half = jnp.bfloat16
    row_count = blk_u.shape[0]
    col_count = blk_u.shape[1]
    rank = blk_u.shape[2]
    order = blk_u.shape[3]
    held_rows = prow_v.shape[0]
    stacked_v = jnp.concatenate([prow_v, pcol_v], 0)
    solved = jnp.einsum(
        "nrb,kb->nrk",
        stacked_v,
        lax.all_gather(linv, "col", axis=0, tiled=True),
        preferred_element_type=fl,
    ).astype(half)
    row_solved = solved[:held_rows]
    col_solved = solved[held_rows:]
    col_sketch = jnp.einsum("jqb,sb->jqs", pcol_u, omega, preferred_element_type=fl).astype(half)
    row_index = lax.axis_index("row")
    col_index = lax.axis_index("col")
    every_u, every_l = (
        lax.all_gather(prow_u, "col", axis=0, tiled=True),
        lax.all_gather(row_solved, "col", axis=0, tiled=True),
    )
    first_row = row_index * row_count
    near_u = lax.dynamic_slice_in_dim(every_u, first_row, row_count, 0)
    near_l = lax.dynamic_slice_in_dim(every_l, first_row, row_count, 0)
    every_cl, every_q = (
        lax.all_gather(col_solved, "row", axis=0, tiled=True),
        lax.all_gather(col_sketch, "row", axis=0, tiled=True),
    )
    first_col = col_index * col_count
    far_l = lax.dynamic_slice_in_dim(every_cl, first_col, col_count, 0)
    far_q = lax.dynamic_slice_in_dim(every_q, first_col, col_count, 0)
    proj = jnp.einsum("ijrb,qb->ijrq", blk_v, omega, preferred_element_type=fl).astype(half)
    base = jnp.einsum("ijrq,ijrb->ijqb", proj, blk_u, preferred_element_type=fl)
    inner = jnp.einsum("irb,jqb->ijrq", near_l, far_l, preferred_element_type=fl)
    coupled = jnp.einsum(
        "ijrq,jqs->ijrs", inner, far_q.astype(fl), precision=lax.Precision.HIGHEST
    ).astype(half)
    update = jnp.einsum("ijrs,irb->ijsb", coupled, near_u, preferred_element_type=fl)
    columns = lax.axis_size("col")
    count = child_u.shape[0]
    slots = columns * CAP
    dest = child_dest[:, 0]
    positions = jnp.arange(count, dtype=jnp.int32)
    earlier = (dest[:, None] == dest[None, :]) & (positions[:, None] > positions[None, :])
    place = jnp.sum(earlier.astype(jnp.int32), 1)
    target = dest * CAP + place
    select = jnp.arange(slots, dtype=jnp.int32)[:, None] == target[None, :]
    occupied = jnp.any(select, 1)
    labels = jnp.where(occupied, jnp.sum(jnp.where(select, child_block[None, :], 0), 1), -1)
    select_half = select.astype(half)
    packed_u = jnp.einsum("sc,crb->srb", select_half, child_u, preferred_element_type=fl).astype(
        half
    )
    packed_u = packed_u.reshape(columns, CAP, rank, order)
    packed_v = jnp.einsum("sc,crb->srb", select_half, child_v, preferred_element_type=fl).astype(
        half
    )
    packed_v = packed_v.reshape(columns, CAP, rank, order)
    recv_u, recv_v, recv_ids = (
        lax.all_to_all(packed_u, "col", split_axis=0, concat_axis=0, tiled=True),
        lax.all_to_all(packed_v, "col", split_axis=0, concat_axis=0, tiled=True),
        lax.all_to_all(
            labels.reshape(columns, CAP), "col", split_axis=0, concat_axis=0, tiled=True
        ),
    )
    weight = jnp.einsum(
        "srb,qb->srq", recv_v.reshape(slots, rank, order), omega, preferred_element_type=fl
    ).astype(half)
    contrib = jnp.einsum(
        "srq,srb->sqb", weight, recv_u.reshape(slots, rank, order), preferred_element_type=fl
    )
    hits = (
        recv_ids.reshape(slots)[:, None]
        == jnp.arange(row_count * col_count, dtype=jnp.int32)[None, :]
    ).astype(fl)
    added = jnp.einsum("sm,sqb->mqb", hits, contrib, precision=lax.Precision.HIGHEST)
    added = added.reshape(row_count, col_count, rank, order)
    sketch = (base - update + added).astype(half)
    return (sketch, row_solved, col_solved)


def solution(mesh):
    in_specs = (
        P("row", "col", None, None),
        P("row", "col", None, None),
        P("col", None, None),
        P("col", None, None),
        P("row", None, None),
        P("row", None, None),
        P("col", None),
        P(),
        P(("row", "col"), None, None),
        P(("row", "col"), None, None),
        P(("row", "col"), None),
        P(("row", "col")),
    )
    out_specs = (P("row", "col", None, None), P("col", None, None), P("row", None, None))
    return jax.shard_map(body, mesh=mesh, in_specs=in_specs, out_specs=out_specs, check_vma=False)
```

profile of v0, /device:TPU:1, one launch (start us, length us, event | category | flops | bytes accessed | tf_op | source)
XLA Modules:
  0.0 302.6 jit_solution(4076611071548354627)
XLA Ops:
  7.2 21.1 %all_gather.16 = bf16[512,512]{1,0:T(8,128)(2,1)S(1)} all-gather(bf16[32,512]{1,0:T(8,128)(2,1)} %param.18), channel_id=1, replica_groups=mesh['row'=8,'col'=16] {'col'}, dimensions={0}, use_global_device_ids=true | all-gather | bytes 557056 | tf_op jit(solution)/shard_map/all_gather | solution.py:34
  28.3 2.3 convolution_convert_fusion.3
  30.7 0.8 slice.9
  31.5 1.1 slice.8
  32.7 2.0 convolution_convert_fusion.5
  34.7 0.5 all-gather.11.cloned.1.call-update
  35.6 0.7 select_n.31
  36.3 4.7 %all-to-all-start = ((s32[16,1,2]{2,1,0:T(1,128)}), s32[16,1,2]{2,1,0:T(1,128)S(1)}, u32[]{:S(2)}, u32[]{:S(2)}) async-start(s32[16,1,2]{2,1,0:T(1,128)} %bitcast.13), calls=%async_computation | async-start | bytes 16384 | tf_op jit(solution)/shard_map/all_to_all | solution.py:86
  41.0 2.2 convolution_convert_fusion
  43.2 2.8 reshape.59
  46.0 3.3 %copy.42 = bf16[16,2,64,512]{3,1,2,0:T(2,128)(2,1)} copy(bf16[16,2,64,512]{3,1,0,2:T(2,128)(2,1)S(1)} %reshape.59) | data formatting | bytes 4194304 | tf_op jit(solution)/shard_map/reshape | solution.py:78
  49.3 6.6 %all-to-all-start.2 = ((bf16[16,2,64,512]{3,1,2,0:T(2,128)(2,1)}), bf16[16,2,64,512]{3,1,2,0:T(2,128)(2,1)S(1)}, u32[]{:S(2)}, u32[]{:S(2)}) async-start(bf16[16,2,64,512]{3,1,2,0:T(2,128)(2,1)} %copy.42), calls=%async_computation.2 | async-start | bytes 4194304 | tf_op jit(solution)/shard_map/all_to_all | solution.py:84
  56.0 2.2 convolution_convert_fusion.1
  58.2 4.1 %reshape.57 = bf16[16,2,64,512]{3,1,0,2:T(2,128)(2,1)} reshape(bf16[32,64,512]{2,0,1:T(8,128)(2,1)} %convolution_convert_fusion.1) | data formatting | bytes 4194304 | tf_op jit(solution)/shard_map/reshape | solution.py:82
  62.3 4.8 %copy.39 = bf16[16,2,64,512]{3,1,2,0:T(2,128)(2,1)} copy(bf16[16,2,64,512]{3,1,0,2:T(2,128)(2,1)} %reshape.57) | data formatting | bytes 4194304 | tf_op jit(solution)/shard_map/reshape | solution.py:82
  67.2 11.4 %all-to-all-done.2 = bf16[16,2,64,512]{3,1,2,0:T(2,128)(2,1)S(1)} async-done(((bf16[16,2,64,512]{3,1,2,0:T(2,128)(2,1)}), bf16[16,2,64,512]{3,1,2,0:T(2,128)(2,1)S(1)}, u32[]{:S(2)}, u32[]{:S(2)}) %all-to-all-start.2) | async-done | bytes 2097184 | tf_op jit(solution)/shard_map/all_to_all | solution.py:84
  78.6 7.2 %all-to-all-start.1 = ((bf16[16,2,64,512]{3,1,2,0:T(2,128)(2,1)}), bf16[16,2,64,512]{3,1,2,0:T(2,128)(2,1)}, u32[]{:S(2)}, u32[]{:S(2)}) async-start(bf16[16,2,64,512]{3,1,2,0:T(2,128)(2,1)} %copy.39), calls=%async_computation.1 | async-start | bytes 4194304 | tf_op jit(solution)/shard_map/all_to_all | solution.py:85
  85.7 0.5 broadcast.23
  86.2 0.7 reduce.3
  87.0 1.8 copy.43
  88.8 34.2 %all-to-all-done.1 = bf16[16,2,64,512]{3,1,2,0:T(2,128)(2,1)} async-done(((bf16[16,2,64,512]{3,1,2,0:T(2,128)(2,1)}), bf16[16,2,64,512]{3,1,2,0:T(2,128)(2,1)}, u32[]{:S(2)}, u32[]{:S(2)}) %all-to-all-start.1) | async-done | bytes 2097184 | tf_op jit(solution)/shard_map/all_to_all | solution.py:85
  123.0 3.4 %copy.40 = bf16[16,2,64,512]{3,2,1,0:T(8,128)(2,1)} copy(bf16[16,2,64,512]{3,1,2,0:T(2,128)(2,1)} %all-to-all-done.1) | data formatting | bytes 4194304 | tf_op jit(solution)/shard_map/all_to_all | solution.py:85
  126.4 5.5 %fusion.12 = f32[32,64,512]{2,1,0:T(8,128)} fusion(bf16[32,64,512]{2,1,0:T(8,128)(2,1)S(1)} %bitcast.60, bf16[32,64,512]{2,1,0:T(8,128)(2,1)} %bitcast.61, bf16[64,512]{1,0:T(8,128)(2,1)S(1)} %copy-done.5), kind=kOutput, calls=%fused_computation.17 | convolution fusion | flops 268566528 | bytes 8454144 | tf_op jit(solution)/shard_map/srq,srb->sqb/dot_general | solution.py:93
  131.9 12.6 %fusion = f32[96,64,512]{2,0,1:T(8,128)} fusion(f32[32,64,512]{2,1,0:T(8,128)} %fusion.12, s32[32]{0:T(128)S(1)} %eq.47), kind=kOutput, calls=%fused_computation.1 | convolution fusion | flops 1207962624 | bytes 16777344 | tf_op jit(solution)/shard_map/sm,sqb->mqb/dot_general | solution.py:100
  144.5 16.4 %copy.46 = f32[96,64,512]{2,1,0:T(8,128)} copy(f32[96,64,512]{2,0,1:T(8,128)} %fusion) | data formatting | bytes 25165824 | tf_op jit(solution)/shard_map/sm,sqb->mqb/dot_general | solution.py:100
  160.9 20.9 %all-gather.7.cloned.1.call-done = bf16[128,64,512]{2,1,0:T(8,128)(2,1)} async-done(((bf16[16,64,512]{2,1,0:T(8,128)(2,1)}), bf16[128,64,512]{2,1,0:T(8,128)(2,1)}) %all-gather.7.cloned.1.call-update) | async-done | bytes 8388624 | tf_op jit(solution)/shard_map/all_gather | solution.py:50
  181.8 4.0 %convolution_bitcast_fusion = f32[12,8,64,64]{2,3,0,1:T(8,128)} fusion(bf16[96,64,512]{2,1,0:T(8,128)(2,1)} %all-gather.9.cloned.1.call-done, s32[]{:T(128)S(6)} %select_n.28, bf16[128,64,512]{2,1,0:T(8,128)(2,1)} %all-gather.7.cloned.1.call-done, s32[]{:T(128)S(6)} %select_n.27), kind=kOutput, calls=%fused_computation.7 | convolution fusion | flops 402653184 | bytes 2883592 | tf_op jit(solution)/shard_map/irb,jqb->ijrq/dot_general | solution.py:58
  185.8 23.1 %all-gather.5.cloned.1.call-done = bf16[128,64,64]{2,1,0:T(8,128)(2,1)} async-done(((bf16[16,64,64]{2,1,0:T(8,128)(2,1)}), bf16[128,64,64]{2,1,0:T(8,128)(2,1)}) %all-gather.5.cloned.1.call-update) | async-done | bytes 1048592 | tf_op jit(solution)/shard_map/all_gather | solution.py:51
  208.9 3.7 %fusion.4 = bf16[8,64,12,64]{3,1,0,2:T(8,128)(2,1)S(1)} fusion(f32[12,8,64,64]{2,3,0,1:T(8,128)} %convolution_bitcast_fusion, bf16[128,64,64]{2,1,0:T(8,128)(2,1)} %all-gather.5.cloned.1.call-done, s32[]{:T(128)S(6)} %select_n.27), kind=kOutput, calls=%fused_computation.9 | convolution fusion | flops 302383104 | bytes 4063236 | tf_op jit(solution)/shard_map/ijrq,jqs->ijrs/dot_general | solution.py:59
  212.6 59.6 %all-gather.11.cloned.1.call-done = bf16[96,64,512]{2,1,0:T(8,128)(2,1)} async-done(((bf16[6,64,512]{2,1,0:T(8,128)(2,1)}), bf16[96,64,512]{2,1,0:T(8,128)(2,1)}) %all-gather.11.cloned.1.call-update) | async-done | bytes 6291472 | tf_op jit(solution)/shard_map/all_gather | solution.py:43
  272.3 7.4 %fusion.7 = f32[12,8,64,512]{3,2,1,0:T(8,128)} fusion(bf16[8,64,12,64]{3,1,0,2:T(8,128)(2,1)S(1)} %fusion.4, bf16[96,64,512]{2,1,0:T(8,128)(2,1)} %all-gather.11.cloned.1.call-done, s32[]{:T(128)S(6)} %select_n.28), kind=kOutput, calls=%fused_computation.11 | convolution fusion | flops 402653184 | bytes 14155780 | tf_op jit(solution)/shard_map/ijrs,irb->ijsb/dot_general | solution.py:62
  279.6 16.4 %add_convert_fusion = bf16[12,8,64,512]{3,2,1,0:T(8,128)(2,1)} fusion(f32[12,8,64,512]{3,2,1,0:T(8,128)} %bitcast.59, f32[12,8,64,512]{3,2,1,0:T(8,128)} %fusion.7, bf16[12,8,64,512]{3,2,1,0:T(8,128)(2,1)} %param.12, bf16[12,8,64,512]{3,2,1,0:T(8,128)(2,1)} %param.13, bf16[64,512]{1,0:T(8,128)(2,1)S(1)} %copy-done.5), kind=kOutput, calls=%fused_computation | convolution fusion | flops 815136768 | bytes 44105728 | tf_op jit(solution)/shard_map/ijrq,ijrb->ijqb/dot_general | solution.py:57
  (31 shorter events, 0.7 us)
Async XLA Ops:
  7.2 33.8 %copy-start = (bf16[16,64,512]{2,1,0:T(8,128)(2,1)S(1)}, bf16[16,64,512]{2,1,0:T(8,128)(2,1)}, u32[]{:S(2)}) copy-start(bf16[16,64,512]{2,1,0:T(8,128)(2,1)} %param.20) | copy-start | bytes 3145732
  7.2 153.7 %all-gather.9.cloned.1.call-start = ((), (), s32[]{:S(2)}) async-start(), calls=%async_computation.5 | async-start | bytes 6684672 | tf_op jit(solution)/shard_map/all_gather | solution.py:44
  30.6 2.0 copy-start.3
  30.6 4.6 %copy-start.6 = (s32[16,1]{0,1:T(1,128)S(1)}, s32[16,1]{0,1:T(1,128)}, u32[]{:S(2)}) copy-start(s32[16,1]{0,1:T(1,128)} %param.22) | copy-start | bytes 196
  30.6 4.9 %copy-start.7 = (s32[16]{0:T(128)S(1)}, s32[16]{0:T(128)}, u32[]{:S(2)}) copy-start(s32[16]{0:T(128)} %param.23) | copy-start | bytes 196
  31.5 150.4 %all-gather.7.cloned.1.call-start = ((), (), s32[]{:S(2)}) async-start(), calls=%async_computation.4 | async-start | bytes 9437184 | tf_op jit(solution)/shard_map/all_gather | solution.py:50
  32.6 176.3 %all-gather.5.cloned.1.call-start = ((), (), s32[]{:S(2)}) async-start(), calls=%async_computation.3 | async-start | bytes 2359296 | tf_op jit(solution)/shard_map/all_gather | solution.py:51
  34.6 237.6 %all-gather.11.cloned.1.call-start = ((), (), s32[]{:S(2)}) async-start(), calls=%async_computation.6 | async-start | bytes 6684672 | tf_op jit(solution)/shard_map/all_gather | solution.py:43
  36.3 13.0 %all-to-all-start = ((s32[16,1,2]{2,1,0:T(1,128)}), s32[16,1,2]{2,1,0:T(1,128)S(1)}, u32[]{:S(2)}, u32[]{:S(2)}) async-start(s32[16,1,2]{2,1,0:T(1,128)} %bitcast.13), calls=%async_computation | async-start | bytes 16384 | tf_op jit(solution)/shard_map/all_to_all | solution.py:86
  46.0 10.0 %copy-start.4 = (bf16[16,64,512]{2,1,0:T(8,128)(2,1)S(1)}, bf16[16,64,512]{2,1,0:T(8,128)(2,1)}, u32[]{:S(2)}) copy-start(bf16[16,64,512]{2,1,0:T(8,128)(2,1)} %param.21) | copy-start | bytes 3145732
  49.3 29.2 %all-to-all-start.2 = ((bf16[16,2,64,512]{3,1,2,0:T(2,128)(2,1)}), bf16[16,2,64,512]{3,1,2,0:T(2,128)(2,1)S(1)}, u32[]{:S(2)}, u32[]{:S(2)}) async-start(bf16[16,2,64,512]{3,1,2,0:T(2,128)(2,1)} %copy.42), calls=%async_computation.2 | async-start | bytes 4194304 | tf_op jit(solution)/shard_map/all_to_all | solution.py:84
  78.6 44.4 %all-to-all-start.1 = ((bf16[16,2,64,512]{3,1,2,0:T(2,128)(2,1)}), bf16[16,2,64,512]{3,1,2,0:T(2,128)(2,1)}, u32[]{:S(2)}, u32[]{:S(2)}) async-start(bf16[16,2,64,512]{3,1,2,0:T(2,128)(2,1)} %copy.39), calls=%async_computation.1 | async-start | bytes 4194304 | tf_op jit(solution)/shard_map/all_to_all | solution.py:85
  88.8 37.6 %copy-start.2 = (bf16[16,2,64,512]{3,2,1,0:T(8,128)(2,1)S(1)}, bf16[16,2,64,512]{3,2,1,0:T(8,128)(2,1)}, u32[]{:S(2)}) copy-start(bf16[16,2,64,512]{3,2,1,0:T(8,128)(2,1)} %copy.43) | copy-start | bytes 6291460
  88.8 37.6 %copy-start.5 = (bf16[64,512]{1,0:T(8,128)(2,1)S(1)}, bf16[64,512]{1,0:T(8,128)(2,1)}, u32[]{:S(2)}) copy-start(bf16[64,512]{1,0:T(8,128)(2,1)} %param.19) | copy-start | bytes 196612
  279.6 16.4 %copy-start.1 = (bf16[16,64,512]{2,1,0:T(8,128)(2,1)S(1)}, bf16[16,64,512]{2,1,0:T(8,128)(2,1)}, u32[]{:S(2)}) copy-start(bf16[16,64,512]{2,1,0:T(8,128)(2,1)} %param.20) | copy-start | bytes 3145732
Sparse Core Ops, SparseCore 0:
  31.6 95.2 all-gather.8
  129.1 52.6 all-gather.6
  183.6 25.3 all-gather.4
  211.0 61.2 all-gather.10
where the time goes:
time: 303 us
  waiting for transfers between devices  150 us (50%)
  matrix products  58.3 us (19%)
  local copies, waits for them, and re-layouts  39.8 us (13%)
  blocking collectives  21.1 us (7%)
  starting transfers between devices  18.6 us (6%)
  between operations  13.9 us (5%)
    all_gather x1, waiting for transfers between devices, body(): lax.all_gather(prow_u, 'col', axis=0, tiled=True)  59.6 us
    all_to_all x1, waiting for transfers between devices, body(): lax.all_to_all(packed_v, 'col', split_axis=0, concat_axis=0, tiled=True)  34.2 us
    all_gather x1, waiting for transfers between devices, body(): lax.all_gather(col_sketch, 'row', axis=0, tiled=True)  23.1 us
    all_gather x1, blocking collectives, body(): lax.all_gather(linv, 'col', axis=0, tiled=True)  21.1 us
    all_gather x1, waiting for transfers between devices, body(): lax.all_gather(col_solved, 'row', axis=0, tiled=True)  20.9 us
    dot_general x1, matrix products, body(): base = jnp.einsum('ijrq,ijrb->ijqb', proj, blk_u, preferred_element_type=fl)  16.4 us
    dot_general x1, local copies, waits for them, and re-layouts, body(): jnp.einsum('sm,sqb->mqb', hits, contrib, precision=lax.Precision.HIGHEST)  16.4 us
    dot_general x1, matrix products, body(): jnp.einsum('sm,sqb->mqb', hits, contrib, precision=lax.Precision.HIGHEST)  12.6 us
  transfers between devices with their start and end apart: 7, of which 5 were waited for; matrix products, arithmetic and copies ran while one was open for 24% of the time, Pallas kernels for 0%

commit v1 on v0

v1 whole, which is shorter than its diff:
```python
import functools

import jax
import jax.numpy as jnp
from jax import lax
from jax.experimental import pallas as pl
from jax.experimental.pallas import tpu as pltpu
from jax.sharding import PartitionSpec as P

MESH = pl.DeviceIdType.MESH
HALF = jnp.bfloat16
FULL = jnp.float32
SIDE = 4
ROWS, COLS = 2 * SIDE, SIDE * SIDE
OFFSETS = sorted(
    [(dx, dz) for dx in range(SIDE) for dz in range(SIDE)],
    key=lambda o: (o == (0, 0), min(o[0], SIDE - o[0]) + min(o[1], SIDE - o[1])),
)


def nt(a, b):
    return lax.dot_general(a, b, (((1,), (1,)), ((), ())), preferred_element_type=FULL)


def nn(a, b):
    return lax.dot_general(a, b, (((1,), (0,)), ((), ())), preferred_element_type=FULL)


def block_diagonal(a, rank):
    n = a.shape[1] // rank
    tall = jnp.concatenate([a] * n, 0)
    row = lax.broadcasted_iota(jnp.int32, tall.shape, 0) // rank
    col = lax.broadcasted_iota(jnp.int32, tall.shape, 1) // rank
    return jnp.where(row == col, tall, jnp.zeros_like(tall))


def sketch_of(om, v, u, rank):
    proj = nt(om, v).astype(HALF)
    return nn(block_diagonal(proj, rank), u)


def exchange_kernel(
    blk_u, blk_v, prow_u, prow_v, pcol_u, pcol_v, linv, omega, child_u, child_v, cdest, cblock,
    t_out, rcv, lab, prow_l, pcol_l,
    cu, cv, om, snd, lsnd, lin, pu, pv, bu, bv, pcu, pcv, pcl, pvo, prl, gt,
    local, chs, chr_, las, lar, lis, lir, sib, prs, prr, gs, gr, bsem, tsem,
):
    row, col = lax.axis_index("row"), lax.axis_index("col")
    x, z = col // SIDE, col % SIDE
    y, core = row // 2, row % 2
    rank, order = om.shape
    held = prow_v.shape[0]
    half_rows = linv.shape[0] // 2
    count = child_u.shape[0]
    rows, cols = blk_u.shape[0], blk_u.shape[1]

    def dev(x, y, z, core):
        return (2 * (y % SIDE) + core % 2, SIDE * (x % SIDE) + z % SIDE)

    sibling = dev(x, y, z, 1 - core)

    def remote(src, dst, send, recv, to):
        return pltpu.make_async_remote_copy(
            src_ref=src, dst_ref=dst, send_sem=send, recv_sem=recv, device_id=to,
            device_id_type=MESH,
        )

    first = [
        pltpu.make_async_copy(child_v, cv, local.at[0]),
        pltpu.make_async_copy(child_u, cu, local.at[1]),
        pltpu.make_async_copy(omega, om, local.at[2]),
        pltpu.make_async_copy(
            linv.at[pl.ds(half_rows * core, half_rows)], lin.at[col, core], local.at[3]
        ),
    ]
    for copy in first:
        copy.start()

    to_z = (z + y - x + SIDE) % SIDE
    targets = [(x + core + 2 * i) % SIDE for i in range(2)]
    to_self = [
        (t == x) & (x == y) & (to_z == z) & (z // 2 == core) for t in targets
    ]
    sources = []
    for e in range(2):
        sz = 2 * core + e
        sources.append((y, (y + z - sz + SIDE) % SIDE, sz, (x - y + SIDE) % 2))
    from_self = [
        (s[0] == x) & (s[1] == y) & (s[2] == z) & (s[3] == core) for s in sources
    ]

    barrier = pltpu.get_barrier_semaphore()

    def greet(to):
        pl.semaphore_signal(barrier, 1, device_id=to, device_id_type=MESH)

    for dx, dz in OFFSETS[:-1]:
        greet(dev(x + dx, y, z + dz, core))
    for dy in range(SIDE):
        for dc in range(2):
            if dy or dc:
                greet(dev(x, y + dy, z, core + dc))
    awaited = COLS - 1 + ROWS - 1
    for i in range(2):
        @pl.when(jnp.logical_not(to_self[i]))
        def _():
            greet(dev(targets[i], x, to_z, z // 2))

        @pl.when(jnp.logical_not(from_self[i]))
        def _():
            greet(dev(*sources[i]))

        awaited += 2 - to_self[i].astype(jnp.int32) - from_self[i].astype(jnp.int32)
    pl.semaphore_wait(barrier, awaited)

    lin_copies = []
    for o, (dx, dz) in enumerate(OFFSETS[:-1]):
        copy = remote(
            linv.at[pl.ds(half_rows * core, half_rows)], lin.at[col, core],
            lis.at[o], lir.at[o], dev(x + dx, y, z + dz, core),
        )
        copy.start()
        lin_copies.append(copy)

    place = held * (z % 2)

    def panel_copy(i, a, which):
        src, dst = ((prow_u, pu), (prow_v, pv))[which]
        return remote(
            src, dst.at[pl.ds(place, held)], prs.at[2 * i + which], prr.at[2 * (z % 2) + which], a
        )

    for i in range(2):
        for which in range(2):
            @pl.when(jnp.logical_not(to_self[i]))
            def _():
                panel_copy(i, dev(targets[i], x, to_z, z // 2), which).start()

            @pl.when(to_self[i])
            def _():
                src, dst = ((prow_u, pu), (prow_v, pv))[which]
                pltpu.make_async_copy(
                    src, dst.at[pl.ds(place, held)], prs.at[2 * i + which]
                ).start()

    for copy in first[:3]:
        copy.wait()
    lane = lax.broadcasted_iota(jnp.int32, lsnd.shape[1:], 1)
    child_copies = []
    for o, (dx, dz) in enumerate(OFFSETS):
        dest = SIDE * ((x + dx) % SIDE) + (z + dz) % SIDE

        def find(c, found, dest=dest):
            one, two = found
            hit = cdest[c, 0] == dest
            two = jnp.where(hit & (one >= 0), c, two)
            one = jnp.where(hit & (one < 0), c, one)
            return one, two

        one, two = lax.fori_loop(0, count, find, (jnp.int32(-1), jnp.int32(-1)))
        label_one = jnp.where(one >= 0, cblock[jnp.maximum(one, 0)], -1)
        label_two = jnp.where(two >= 0, cblock[jnp.maximum(two, 0)], -1)
        one, two = jnp.maximum(one, 0), jnp.maximum(two, 0)
        lsnd[o] = jnp.where(lane == 0, label_one, label_two)
        v = jnp.concatenate([cv[one], cv[two]], 0)
        u = jnp.concatenate([cu[one], cu[two]], 0)
        snd[o] = sketch_of(om[...], v, u, rank).astype(HALF)
        if (dx, dz) == (0, 0):
            copies = [
                pltpu.make_async_copy(snd.at[o], rcv.at[col], chs.at[o]),
                pltpu.make_async_copy(lsnd.at[o], lab.at[col], las.at[o]),
            ]
        else:
            to = dev(x + dx, y, z + dz, core)
            copies = [
                remote(snd.at[o], rcv.at[col], chs.at[o], chr_.at[o], to),
                remote(lsnd.at[o], lab.at[col], las.at[o], lar.at[o], to),
            ]
        for copy in copies:
            copy.start()
        child_copies += copies

    second = [
        pltpu.make_async_copy(pcol_v, pcv, local.at[4]),
        pltpu.make_async_copy(prow_v, pvo, local.at[5]),
        pltpu.make_async_copy(pcol_u, pcu, local.at[6]),
    ]
    for copy in second:
        copy.start()

    def block_copies(i):
        return (
            pltpu.make_async_copy(blk_u.at[i], bu.at[i], bsem.at[0, i]),
            pltpu.make_async_copy(blk_v.at[i], bv.at[i], bsem.at[1, i]),
        )

    for i in range(rows):
        for copy in block_copies(i):
            copy.start()

    first[3].wait()
    for copy in lin_copies:
        copy.wait_recv()
    share = remote(lin.at[:, core], lin.at[:, core], sib.at[0], sib.at[1], sibling)
    share.start()
    share.wait_recv()

    inverse = lin[...].reshape(order, order)
    for copy in second:
        copy.wait()
    piece = 4
    for j in range(0, pcol_v.shape[0], piece):
        part = pcv[j : j + piece].reshape(piece * rank, order)
        pcl[j : j + piece] = nt(part, inverse).astype(HALF).reshape(piece, rank, order)
    prl[...] = nt(pvo[...].reshape(held * rank, order), inverse).astype(HALF).reshape(prl.shape)
    solved = [
        pltpu.make_async_copy(pcl, pcol_l, local.at[7]),
        pltpu.make_async_copy(prl, prow_l, local.at[8]),
    ]
    for copy in solved:
        copy.start()

    def g_remote(h, dy, dc_core, recv):
        return remote(
            gt.at[h], gt.at[h], gs.at[2 * dy + h], gr.at[recv], dev(x, y + dy, z, dc_core)
        )

    source = (y == x) & (core == z // 2)

    @pl.when(source)
    def _():
        base = cols * (z % 2)
        for h in range(2):
            j = base + 4 * h
            qu = pcu[pl.ds(j, 4)].reshape(4 * rank, order)
            cl = pcl[pl.ds(j, 4)].reshape(4 * rank, order)
            gt[h] = sketch_of(om[...], qu, cl, rank).astype(HALF)
            for dy in (1, 3, 2):
                g_remote(h, dy, h, 0).start()
            g_remote(h, 0, 1 - core, (core + h + 1) % 2).start()

    @pl.when(jnp.logical_not(source))
    def _():
        remote(gt.at[core], gt.at[core], gs.at[0], gr.at[0], sibling).wait_recv()

    @pl.when(y != x)
    def _():
        remote(gt.at[core], gt.at[core], gs.at[0], gr.at[1], sibling).start()

    @pl.when(jnp.logical_not(source))
    def _():
        remote(gt.at[1 - core], gt.at[1 - core], gs.at[0], gr.at[1], sibling).wait_recv()

    for e in range(2):
        for which in range(2):
            src, dst = ((prow_u, pu), (prow_v, pv))[which]
            into = dst.at[pl.ds(held * e, held)]

            @pl.when(jnp.logical_not(from_self[e]))
            def _():
                remote(src, into, prs.at[0], prr.at[2 * e + which], sibling).wait_recv()

    for i in range(2):
        for which in range(2):
            src, dst = ((prow_u, pu), (prow_v, pv))[which]

            @pl.when(to_self[i])
            def _():
                pltpu.make_async_copy(
                    src, dst.at[pl.ds(place, held)], prs.at[2 * i + which]
                ).wait()

    lanes = lax.broadcasted_iota(jnp.int32, (cols * rank, 2 * rank), 1)

    def pair(ii, carry):
        near_v = pv[pl.ds(2 * ii, 2)].reshape(2 * rank, order)
        near_u = pu[pl.ds(2 * ii, 2)].reshape(2 * rank, order)
        near_l = nt(near_v, lin[...].reshape(order, order)).astype(HALF)
        coupled = nt(gt[...].reshape(cols * rank, order), near_l).astype(HALF)
        for b in range(2):
            i = 2 * ii + b
            for copy in block_copies(i):
                copy.wait()
            mine = jnp.where(lanes // rank == b, coupled, jnp.zeros_like(coupled))
            for h in range(2):
                v = bv[i, 4 * h : 4 * h + 4].reshape(4 * rank, order)
                u = bu[i, 4 * h : 4 * h + 4].reshape(4 * rank, order)
                part = sketch_of(om[...], v, u, rank)
                part = part - nn(mine[4 * rank * h : 4 * rank * (h + 1)], near_u)
                bv[i, 4 * h : 4 * h + 4] = part.astype(HALF).reshape(4, rank, order)
            pltpu.make_async_copy(bv.at[i], t_out.at[i], tsem.at[i]).start()
        return carry

    lax.fori_loop(0, rows // 2, pair, 0)

    for i in range(rows):
        pltpu.make_async_copy(bv.at[i], t_out.at[i], tsem.at[i]).wait()
    for copy in solved:
        copy.wait()
    for copy in lin_copies:
        copy.wait_send()
    share.wait_send()

    @pl.when(source)
    def _():
        for h in range(2):
            for dy in (1, 3, 2):
                g_remote(h, dy, h, 0).wait_send()
            g_remote(h, 0, 1 - core, 0).wait_send()

    @pl.when(y != x)
    def _():
        remote(gt.at[core], gt.at[core], gs.at[0], gr.at[1], sibling).wait_send()

    for i in range(2):
        for which in range(2):
            @pl.when(jnp.logical_not(to_self[i]))
            def _():
                panel_copy(i, dev(targets[i], x, to_z, z // 2), which).wait_send()

    for copy in child_copies:
        copy.wait()


def finish_kernel(
    t_in, rcv, lab, prow_in, pcol_in, sketch, prow_l, pcol_l,
    tv, rv, head, following, tsem, osem, sems,
):
    rows, cols = t_in.shape[0], t_in.shape[1]
    slots = rcv.shape[0]
    loads = [pltpu.make_async_copy(rcv, rv, sems.at[0])]
    passed = [
        pltpu.make_async_copy(prow_in, prow_l, sems.at[1]),
        pltpu.make_async_copy(pcol_in, pcol_l, sems.at[2]),
    ]

    def load(i):
        return pltpu.make_async_copy(t_in.at[i], tv.at[i], tsem.at[i])

    def store(i):
        return pltpu.make_async_copy(tv.at[i], sketch.at[i], osem.at[i])

    load(0).start()
    loads[0].start()
    for i in range(1, rows):
        load(i).start()
    for copy in passed:
        copy.start()

    def clear(m, carry):
        head[m] = -1
        return carry

    lax.fori_loop(0, rows * cols, clear, 0, unroll=8)

    def link(s, carry):
        label = lab[s // 2, 0, s % 2]

        @pl.when(label >= 0)
        def _():
            following[s] = head[label]
            head[label] = s

        return carry

    lax.fori_loop(0, slots, link, 0)
    loads[0].wait()

    def one_row(i, carry):
        load(i).wait()

        def one_block(j, carry):
            slot = head[i * cols + j]

            @pl.when(slot >= 0)
            def _():
                def add(state):
                    s, total = state
                    return following[s], total + rv[s].astype(FULL)

                _, total = lax.while_loop(
                    lambda state: state[0] >= 0, add, (slot, tv[i, j].astype(FULL))
                )
                tv[i, j] = total.astype(HALF)

            return carry

        lax.fori_loop(0, cols, one_block, 0)
        store(i).start()
        return carry

    lax.fori_loop(0, rows, one_row, 0)
    for i in range(rows):
        store(i).wait()
    for copy in passed:
        copy.wait()


def body(
    blk_u, blk_v, prow_u, prow_v, pcol_u, pcol_v, linv, omega, child_u, child_v, child_dest,
    child_block,
):
    rows, cols, rank, order = blk_u.shape
    held, held_cols, count = prow_u.shape[0], pcol_u.shape[0], child_u.shape[0]
    anywhere = pl.BlockSpec(memory_space=pl.ANY)
    scalars = pl.BlockSpec(memory_space=pltpu.SMEM)
    dma = pltpu.SemaphoreType.DMA

    def half(*shape):
        return pltpu.VMEM(shape, HALF)

    partial, received, labels, row_solved, col_solved = pl.pallas_call(
        exchange_kernel,
        out_shape=(
            jax.ShapeDtypeStruct(blk_u.shape, HALF),
            jax.ShapeDtypeStruct((COLS, 2 * rank, order), HALF),
            jax.ShapeDtypeStruct((COLS, 8, 128), jnp.int32),
            jax.ShapeDtypeStruct(prow_v.shape, HALF),
            jax.ShapeDtypeStruct(pcol_v.shape, HALF),
        ),
        in_specs=[anywhere] * 10 + [scalars] * 2,
        out_specs=(anywhere,) * 5,
        scratch_shapes=[
            half(count, rank, order),
            half(count, rank, order),
            half(rank, order),
            half(COLS, 2 * rank, order),
            pltpu.VMEM((COLS, 8, 128), jnp.int32),
            half(COLS, 2, linv.shape[0] // 2, order),
            half(rows, rank, order),
            half(rows, rank, order),
            half(*blk_u.shape),
            half(*blk_v.shape),
            half(held_cols, rank, order),
            half(held_cols, rank, order),
            half(held_cols, rank, order),
            half(held, rank, order),
            half(held, rank, order),
            half(2, cols * rank // 2, order),
            dma((9,)),
            dma((COLS,)),
            dma((COLS,)),
            dma((COLS,)),
            dma((COLS,)),
            dma((COLS,)),
            dma((COLS,)),
            dma((2,)),
            dma((4,)),
            dma((4,)),
            dma((8,)),
            dma((2,)),
            dma((2, rows)),
            dma((rows,)),
        ],
        compiler_params=pltpu.CompilerParams(
            collective_id=0, has_side_effects=True, vmem_limit_bytes=52 * 2**20
        ),
        name="exchange",
    )(
        blk_u, blk_v, prow_u, prow_v, pcol_u, pcol_v, linv, omega, child_u, child_v, child_dest,
        child_block,
    )
    return pl.pallas_call(
        finish_kernel,
        out_shape=(
            jax.ShapeDtypeStruct(blk_u.shape, HALF),
            jax.ShapeDtypeStruct(prow_v.shape, HALF),
            jax.ShapeDtypeStruct(pcol_v.shape, HALF),
        ),
        in_specs=[anywhere, anywhere, scalars, anywhere, anywhere],
        out_specs=(anywhere,) * 3,
        scratch_shapes=[
            half(*blk_u.shape),
            half(2 * COLS, rank, order),
            pltpu.SMEM((rows * cols,), jnp.int32),
            pltpu.SMEM((2 * COLS,), jnp.int32),
            dma((rows,)),
            dma((rows,)),
            dma((3,)),
        ],
        compiler_params=pltpu.CompilerParams(vmem_limit_bytes=32 * 2**20),
        name="finish",
    )(partial, received.reshape(2 * COLS, rank, order), labels, row_solved, col_solved)


def solution(mesh):
    in_specs = (
        P("row", "col", None, None),
        P("row", "col", None, None),
        P("col", None, None),
        P("col", None, None),
        P("row", None, None),
        P("row", None, None),
        P("col", None),
        P(),
        P(("row", "col"), None, None),
        P(("row", "col"), None, None),
        P(("row", "col"), None),
        P(("row", "col")),
    )
    out_specs = (P("row", "col", None, None), P("col", None, None), P("row", None, None))
    return jax.shard_map(body, mesh=mesh, in_specs=in_specs, out_specs=out_specs, check_vma=False)
```

time: 303 us -> 90.6 us (0.30)
  the two profiles are of different devices: /device:TPU:1 before, /device:TPU:14 now
where the time goes in v1:
time: 90.6 us; the launch traced here: 90.2 us
  Pallas kernels  79 us (87%)
  local copies, waits for them, and re-layouts  10.6 us (12%)
    pallas_call x1, Pallas kernels, body(): pl.pallas_call(exchange_kernel, out_shape=(jax.ShapeDtypeStruct(blk_u.sha...  73 us
    unnamed x17, local copies, waits for them, and re-layouts  10.6 us
    pallas_call x1, Pallas kernels, body(): pl.pallas_call(finish_kernel, out_shape=(jax.ShapeDtypeStruct(blk_u.shape...  5.97 us

profile of v1, /device:TPU:14, one launch (start us, length us, event | category | flops | bytes accessed | tf_op | source)
XLA Modules:
  0.0 90.2 jit_solution(4766666532230990431)
XLA Ops:
  0.6 0.7 copy.15.cdest
  1.4 0.0 copy-start.3
  1.4 1.0 %copy-done.3 = bf16[6,64,512]{2,1,0:T(8,128)(2,1)S(1)} copy-done((bf16[6,64,512]{2,1,0:T(8,128)(2,1)S(1)}, bf16[6,64,512]{2,1,0:T(8,128)(2,1)}, u32[]{:S(2)}) %copy-start.3) | copy-done | bytes 393240
  2.4 0.0 copy-start.4
  2.4 1.0 %copy-done.4 = bf16[6,64,512]{2,1,0:T(8,128)(2,1)S(1)} copy-done((bf16[6,64,512]{2,1,0:T(8,128)(2,1)S(1)}, bf16[6,64,512]{2,1,0:T(8,128)(2,1)}, u32[]{:S(2)}) %copy-start.4) | copy-done | bytes 393240
  3.4 0.0 copy-start.5
  3.4 0.8 copy-done.5
  4.2 0.0 copy-start.6
  4.2 0.8 copy-done.6
  5.0 0.0 copy-start.7
  5.0 0.7 copy-done.7
  5.6 73.0 %exchange.1 = (bf16[12,8,64,512]{3,2,1,0:T(8,128)(2,1)}, bf16[16,128,512]{2,1,0:T(8,128)(2,1)}, s32[16,8,128]{2,1,0:T(8,128)S(1)}, bf16[6,64,512]{2,1,0:T(8,128)(2,1)S(1)}, bf16[16,64,512]{2,1,0:T(8,128)(2,1)}) custom-call(bf16[12,8,64,512]{3,2,1,0:T(8,128)(2,1)} %blk_u.1, bf16[12,8,64,512]{3,2,1,0:T(8,128)(2,1)} %blk_v.1, ...), custom_call_target="tpu_custom_call" | custom-call | tf_op jit(solution)/shard_map/exchange/pallas_call | solution.py:412
  78.6 0.0 copy-start
  78.6 2.8 %copy-done = bf16[12,8,64,512]{3,2,1,0:T(8,128)(2,1)S(1)} copy-done((bf16[12,8,64,512]{3,2,1,0:T(8,128)(2,1)S(1)}, bf16[12,8,64,512]{3,2,1,0:T(8,128)(2,1)}, u32[]{:S(2)}) %copy-start) | copy-done | bytes 6291480
  81.4 0.0 copy-start.1
  81.4 1.6 %copy-done.1 = bf16[16,128,512]{2,1,0:T(8,128)(2,1)S(1)} copy-done((bf16[16,128,512]{2,1,0:T(8,128)(2,1)S(1)}, bf16[16,128,512]{2,1,0:T(8,128)(2,1)}, u32[]{:S(2)}) %copy-start.1) | copy-done | bytes 2097176
  83.0 0.0 copy-start.2
  83.0 1.2 %copy-done.2 = bf16[16,64,512]{2,1,0:T(8,128)(2,1)S(1)} copy-done((bf16[16,64,512]{2,1,0:T(8,128)(2,1)S(1)}, bf16[16,64,512]{2,1,0:T(8,128)(2,1)}, u32[]{:S(2)}) %copy-start.2) | copy-done | bytes 1048600
  84.2 6.0 %finish.1 = (bf16[12,8,64,512]{3,2,1,0:T(8,128)(2,1)}, bf16[6,64,512]{2,1,0:T(8,128)(2,1)}, bf16[16,64,512]{2,1,0:T(8,128)(2,1)}) custom-call(bf16[12,8,64,512]{3,2,1,0:T(8,128)(2,1)S(1)} %copy-done, bf16[32,64,512]{2,1,0:T(8,128)(2,1)S(1)} %bitcast.1, s32[16,8,128]{2,1,0:T(8,128)S(1)} %get-tuple-element.10.lab, ...), custom_call_target="tpu_custom_call" | custom-call | tf_op jit(solution)/shard_map/finish/pallas_call | solution.py:463
Async XLA Ops:
  1.4 1.0 %copy-start.3 = (bf16[6,64,512]{2,1,0:T(8,128)(2,1)S(1)}, bf16[6,64,512]{2,1,0:T(8,128)(2,1)}, u32[]{:S(2)}) copy-start(bf16[6,64,512]{2,1,0:T(8,128)(2,1)} %prow_u.1) | copy-start | bytes 1179652
  2.4 1.0 %copy-start.4 = (bf16[6,64,512]{2,1,0:T(8,128)(2,1)S(1)}, bf16[6,64,512]{2,1,0:T(8,128)(2,1)}, u32[]{:S(2)}) copy-start(bf16[6,64,512]{2,1,0:T(8,128)(2,1)} %prow_v.1) | copy-start | bytes 1179652
  3.4 0.8 copy-start.5
  4.2 0.8 copy-start.6
  5.0 0.7 copy-start.7
  78.6 2.8 %copy-start = (bf16[12,8,64,512]{3,2,1,0:T(8,128)(2,1)S(1)}, bf16[12,8,64,512]{3,2,1,0:T(8,128)(2,1)}, u32[]{:S(2)}) copy-start(bf16[12,8,64,512]{3,2,1,0:T(8,128)(2,1)} %get-tuple-element.8.t_in) | copy-start | bytes 18874372
  81.4 1.6 %copy-start.1 = (bf16[16,128,512]{2,1,0:T(8,128)(2,1)S(1)}, bf16[16,128,512]{2,1,0:T(8,128)(2,1)}, u32[]{:S(2)}) copy-start(bf16[16,128,512]{2,1,0:T(8,128)(2,1)} %get-tuple-element.9) | copy-start | bytes 6291460
  83.0 1.2 %copy-start.2 = (bf16[16,64,512]{2,1,0:T(8,128)(2,1)S(1)}, bf16[16,64,512]{2,1,0:T(8,128)(2,1)}, u32[]{:S(2)}) copy-start(bf16[16,64,512]{2,1,0:T(8,128)(2,1)} %get-tuple-element.12.pcol_in) | copy-start | bytes 3145732

commit v2 on v1

--- a/solution.py
+++ b/solution.py
@@ -40,10 +40,10 @@
 
 
 def exchange_kernel(
-    blk_u, blk_v, prow_u, prow_v, pcol_u, pcol_v, linv, omega, child_u, child_v, cdest, cblock,
+    blk_u, blk_v, prow_u, prow_v, pcol_u, pcol_v, linv, omega, child_u, child_v, child_dest, child_block,
     t_out, rcv, lab, prow_l, pcol_l,
     cu, cv, om, snd, lsnd, lin, pu, pv, bu, bv, pcu, pcv, pcl, pvo, prl, gt,
-    local, chs, chr_, las, lar, lis, lir, sib, prs, prr, gs, gr, bsem, tsem,
+    vq, cdest, cblock, local, chs, chr_, las, lar, lis, lir, sib, us, ur, vs, vr, gs, gr, bsem, tsem,
 ):
     row, col = lax.axis_index("row"), lax.axis_index("col")
     x, z = col // SIDE, col % SIDE
@@ -73,21 +73,12 @@
             linv.at[pl.ds(half_rows * core, half_rows)], lin.at[col, core], local.at[3]
         ),
     ]
-    for copy in first:
+    scalar_copies = [
+        pltpu.make_async_copy(child_dest, cdest, local.at[9]),
+        pltpu.make_async_copy(child_block, cblock, local.at[10]),
+    ]
+    for copy in scalar_copies + first:
         copy.start()
-
-    to_z = (z + y - x + SIDE) % SIDE
-    targets = [(x + core + 2 * i) % SIDE for i in range(2)]
-    to_self = [
-        (t == x) & (x == y) & (to_z == z) & (z // 2 == core) for t in targets
-    ]
-    sources = []
-    for e in range(2):
-        sz = 2 * core + e
-        sources.append((y, (y + z - sz + SIDE) % SIDE, sz, (x - y + SIDE) % 2))
-    from_self = [
-        (s[0] == x) & (s[1] == y) & (s[2] == z) & (s[3] == core) for s in sources
-    ]
 
     barrier = pltpu.get_barrier_semaphore()
 
@@ -96,21 +87,28 @@
 
     for dx, dz in OFFSETS[:-1]:
         greet(dev(x + dx, y, z + dz, core))
-    for dy in range(SIDE):
-        for dc in range(2):
-            if dy or dc:
-                greet(dev(x, y + dy, z, core + dc))
-    awaited = COLS - 1 + ROWS - 1
-    for i in range(2):
-        @pl.when(jnp.logical_not(to_self[i]))
-        def _():
-            greet(dev(targets[i], x, to_z, z // 2))
-
-        @pl.when(jnp.logical_not(from_self[i]))
-        def _():
-            greet(dev(*sources[i]))
-
-        awaited += 2 - to_self[i].astype(jnp.int32) - from_self[i].astype(jnp.int32)
+    greet(sibling)
+    source = (y == x) & (core == z // 2)
+    to_self = x == y
+    awaited = COLS + 1 + jnp.where(source, 2 * (SIDE - 1), 0) - jnp.where(to_self, 3, 0)
+    awaited += 2 * SIDE
+
+    @pl.when(source)
+    def _():
+        for dy in range(1, SIDE):
+            for dc in range(2):
+                greet(dev(x, y + dy, z, dc))
+
+    @pl.when(y != x)
+    def _():
+        greet(dev(x, x, z, z // 2))
+
+    for i in range(SIDE):
+        @pl.when(jnp.logical_not(to_self & (i == x)))
+        def _():
+            greet(dev(i, x, z, core))
+            greet(dev(y, i, z, core))
+
     pl.semaphore_wait(barrier, awaited)
 
     lin_copies = []
@@ -122,37 +120,86 @@
         copy.start()
         lin_copies.append(copy)
 
-    place = held * (z % 2)
-
-    def panel_copy(i, a, which):
-        src, dst = ((prow_u, pu), (prow_v, pv))[which]
+    place = pl.ds(held * (z % 2), held)
+    fourth = rank // SIDE
+    quarter = pl.ds(fourth * y, fourth)
+    keeper = core == z // 2
+
+    def u_first(i):
         return remote(
-            src, dst.at[pl.ds(place, held)], prs.at[2 * i + which], prr.at[2 * (z % 2) + which], a
-        )
-
-    for i in range(2):
-        for which in range(2):
-            @pl.when(jnp.logical_not(to_self[i]))
+            prow_u.at[:, quarter], pu.at[place, quarter], us.at[i], ur.at[y], dev(i, x, z, core)
+        )
+
+    def u_second(dz):
+        return remote(
+            pu.at[place], pu.at[place], us.at[SIDE + dz], ur.at[SIDE + z % 2],
+            dev(x, y, z + dz, core),
+        )
+
+    def v_first(dz):
+        return remote(
+            prow_v.at[:, quarter], vq.at[place], vs.at[SIDE + dz], vr.at[SIDE + z % 2],
+            dev(x, y, z + dz, core),
+        )
+
+    def v_second(i):
+        return remote(vq, pv.at[:, quarter], vs.at[i], vr.at[y], dev(i, x, z, core))
+
+    def unless_self(i):
+        return pl.when(jnp.logical_not(to_self & (i == x)))
+
+    @pl.when(keeper)
+    def _():
+        for dz in (1, 3, 2):
+            v_first(dz).start()
+        pltpu.make_async_copy(prow_v.at[:, quarter], vq.at[place], vr.at[SIDE + z % 2]).start()
+        for i in range(SIDE):
+            @unless_self(i)
             def _():
-                panel_copy(i, dev(targets[i], x, to_z, z // 2), which).start()
-
-            @pl.when(to_self[i])
+                u_first(i).start()
+
+        @pl.when(to_self)
+        def _():
+            pltpu.make_async_copy(
+                prow_u.at[:, quarter], pu.at[place, quarter], ur.at[y]
+            ).start()
+
+    def pass_v():
+        for e in range(2):
+            mine = vq.at[pl.ds(held * e, held)]
+            remote(mine, mine, vs.at[0], vr.at[SIDE + e], sibling).wait_recv()
+        for i in range(SIDE):
+            @unless_self(i)
             def _():
-                src, dst = ((prow_u, pu), (prow_v, pv))[which]
-                pltpu.make_async_copy(
-                    src, dst.at[pl.ds(place, held)], prs.at[2 * i + which]
-                ).start()
-
-    for copy in first[:3]:
+                v_second(i).start()
+
+        @pl.when(to_self)
+        def _():
+            pltpu.make_async_copy(vq, pv.at[:, quarter], vr.at[y]).start()
+
+    def pass_u():
+        @pl.when(keeper)
+        def _():
+            for q in range(SIDE):
+                mine = pu.at[place, pl.ds(fourth * q, fourth)]
+                remote(mine, mine, us.at[0], ur.at[q], sibling).wait_recv()
+            for dz in (1, 3, 2):
+                u_second(dz).start()
+
+    for copy in scalar_copies + first[:3]:
         copy.wait()
     lane = lax.broadcasted_iota(jnp.int32, lsnd.shape[1:], 1)
     child_copies = []
     for o, (dx, dz) in enumerate(OFFSETS):
+        if o == 2:
+            pass_v()
+        if o == 4:
+            pass_u()
         dest = SIDE * ((x + dx) % SIDE) + (z + dz) % SIDE
 
         def find(c, found, dest=dest):
             one, two = found
-            hit = cdest[c, 0] == dest
+            hit = cdest[c] == dest
             two = jnp.where(hit & (one >= 0), c, two)
             one = jnp.where(hit & (one < 0), c, one)
             return one, two
@@ -225,8 +272,6 @@
             gt.at[h], gt.at[h], gs.at[2 * dy + h], gr.at[recv], dev(x, y + dy, z, dc_core)
         )
 
-    source = (y == x) & (core == z // 2)
-
     @pl.when(source)
     def _():
         base = cols * (z % 2)
@@ -252,23 +297,15 @@
         remote(gt.at[1 - core], gt.at[1 - core], gs.at[0], gr.at[1], sibling).wait_recv()
 
     for e in range(2):
-        for which in range(2):
-            src, dst = ((prow_u, pu), (prow_v, pv))[which]
-            into = dst.at[pl.ds(held * e, held)]
-
-            @pl.when(jnp.logical_not(from_self[e]))
-            def _():
-                remote(src, into, prs.at[0], prr.at[2 * e + which], sibling).wait_recv()
-
-    for i in range(2):
-        for which in range(2):
-            src, dst = ((prow_u, pu), (prow_v, pv))[which]
-
-            @pl.when(to_self[i])
-            def _():
-                pltpu.make_async_copy(
-                    src, dst.at[pl.ds(place, held)], prs.at[2 * i + which]
-                ).wait()
+        mine = pu.at[pl.ds(held * e, held)]
+
+        @pl.when(jnp.logical_not(keeper & (e == z % 2)))
+        def _():
+            remote(mine, mine, us.at[0], ur.at[SIDE + e], sibling).wait_recv()
+
+    for q in range(SIDE):
+        mine = pv.at[:, pl.ds(fourth * q, fourth)]
+        remote(mine, mine, vs.at[0], vr.at[q], sibling).wait_recv()
 
     lanes = lax.broadcasted_iota(jnp.int32, (cols * rank, 2 * rank), 1)
 
@@ -312,38 +349,35 @@
     def _():
         remote(gt.at[core], gt.at[core], gs.at[0], gr.at[1], sibling).wait_send()
 
-    for i in range(2):
-        for which in range(2):
-            @pl.when(jnp.logical_not(to_self[i]))
+    @pl.when(keeper)
+    def _():
+        for dz in (1, 3, 2):
+            v_first(dz).wait_send()
+            u_second(dz).wait_send()
+        for i in range(SIDE):
+            @unless_self(i)
             def _():
-                panel_copy(i, dev(targets[i], x, to_z, z // 2), which).wait_send()
+                u_first(i).wait_send()
+
+    for i in range(SIDE):
+        @unless_self(i)
+        def _():
+            v_second(i).wait_send()
 
     for copy in child_copies:
         copy.wait()
 
 
 def finish_kernel(
-    t_in, rcv, lab, prow_in, pcol_in, sketch, prow_l, pcol_l,
-    tv, rv, head, following, tsem, osem, sems,
+    partial, rcv, lab, prow_in, pcol_in, sketch, prow_l, pcol_l, fixed, head, following, osem, sems,
 ):
-    rows, cols = t_in.shape[0], t_in.shape[1]
-    slots = rcv.shape[0]
-    loads = [pltpu.make_async_copy(rcv, rv, sems.at[0])]
+    rows, cols = partial.shape[0], partial.shape[1]
+    slots = 2 * rcv.shape[0]
+    rank = partial.shape[2]
     passed = [
-        pltpu.make_async_copy(prow_in, prow_l, sems.at[1]),
-        pltpu.make_async_copy(pcol_in, pcol_l, sems.at[2]),
+        pltpu.make_async_copy(prow_in, prow_l, sems.at[0]),
+        pltpu.make_async_copy(pcol_in, pcol_l, sems.at[1]),
     ]
-
-    def load(i):
-        return pltpu.make_async_copy(t_in.at[i], tv.at[i], tsem.at[i])
-
-    def store(i):
-        return pltpu.make_async_copy(tv.at[i], sketch.at[i], osem.at[i])
-
-    load(0).start()
-    loads[0].start()
-    for i in range(1, rows):
-        load(i).start()
     for copy in passed:
         copy.start()
 
@@ -364,34 +398,35 @@
         return carry
 
     lax.fori_loop(0, slots, link, 0)
-    loads[0].wait()
 
     def one_row(i, carry):
-        load(i).wait()
-
         def one_block(j, carry):
             slot = head[i * cols + j]
+
+            @pl.when(slot < 0)
+            def _():
+                pltpu.make_async_copy(partial.at[i, j], sketch.at[i, j], osem.at[i]).start()
 
             @pl.when(slot >= 0)
             def _():
                 def add(state):
                     s, total = state
-                    return following[s], total + rv[s].astype(FULL)
+                    term = rcv[s // 2, pl.ds(pl.multiple_of(rank * (s % 2), rank), rank)]
+                    return following[s], total + term.astype(FULL)
 
                 _, total = lax.while_loop(
-                    lambda state: state[0] >= 0, add, (slot, tv[i, j].astype(FULL))
+                    lambda state: state[0] >= 0, add, (slot, partial[i, j].astype(FULL))
                 )
-                tv[i, j] = total.astype(HALF)
+                fixed[i, j] = total.astype(HALF)
+                pltpu.make_async_copy(fixed.at[i, j], sketch.at[i, j], osem.at[i]).start()
 
             return carry
 
-        lax.fori_loop(0, cols, one_block, 0)
-        store(i).start()
-        return carry
+        return lax.fori_loop(0, cols, one_block, carry)
 
     lax.fori_loop(0, rows, one_row, 0)
     for i in range(rows):
-        store(i).wait()
+        pltpu.make_async_copy(fixed.at[i], sketch.at[i], osem.at[i]).wait()
     for copy in passed:
         copy.wait()
 
@@ -400,9 +435,14 @@
     blk_u, blk_v, prow_u, prow_v, pcol_u, pcol_v, linv, omega, child_u, child_v, child_dest,
     child_block,
 ):
+    arguments = (
+        blk_u, blk_v, prow_u, prow_v, pcol_u, pcol_v, linv, omega, child_u, child_v,
+        child_dest[:, 0], child_block,
+    )
     rows, cols, rank, order = blk_u.shape
     held, held_cols, count = prow_u.shape[0], pcol_u.shape[0], child_u.shape[0]
     anywhere = pl.BlockSpec(memory_space=pl.ANY)
+    inside = pl.BlockSpec(memory_space=pltpu.VMEM)
     scalars = pl.BlockSpec(memory_space=pltpu.SMEM)
     dma = pltpu.SemaphoreType.DMA
 
@@ -412,13 +452,13 @@
     partial, received, labels, row_solved, col_solved = pl.pallas_call(
         exchange_kernel,
         out_shape=(
-            jax.ShapeDtypeStruct(blk_u.shape, HALF),
-            jax.ShapeDtypeStruct((COLS, 2 * rank, order), HALF),
-            jax.ShapeDtypeStruct((COLS, 8, 128), jnp.int32),
-            jax.ShapeDtypeStruct(prow_v.shape, HALF),
-            jax.ShapeDtypeStruct(pcol_v.shape, HALF),
+            pltpu.VMEM(blk_u.shape, HALF),
+            pltpu.VMEM((COLS, 2 * rank, order), HALF),
+            pltpu.VMEM((COLS, 8, 128), jnp.int32),
+            pltpu.VMEM(prow_v.shape, HALF),
+            pltpu.VMEM(pcol_v.shape, HALF),
         ),
-        in_specs=[anywhere] * 10 + [scalars] * 2,
+        in_specs=[anywhere] * 12,
         out_specs=(anywhere,) * 5,
         scratch_shapes=[
             half(count, rank, order),
@@ -437,7 +477,10 @@
             half(held, rank, order),
             half(held, rank, order),
             half(2, cols * rank // 2, order),
-            dma((9,)),
+            half(rows, rank // SIDE, order),
+            pltpu.SMEM(child_block.shape, jnp.int32),
+            pltpu.SMEM(child_block.shape, jnp.int32),
+            dma((11,)),
             dma((COLS,)),
             dma((COLS,)),
             dma((COLS,)),
@@ -445,21 +488,20 @@
             dma((COLS,)),
             dma((COLS,)),
             dma((2,)),
-            dma((4,)),
-            dma((4,)),
+            dma((2 * SIDE,)),
+            dma((SIDE + 2,)),
+            dma((2 * SIDE,)),
+            dma((SIDE + 2,)),
             dma((8,)),
             dma((2,)),
             dma((2, rows)),
             dma((rows,)),
         ],
         compiler_params=pltpu.CompilerParams(
-            collective_id=0, has_side_effects=True, vmem_limit_bytes=52 * 2**20
+            collective_id=0, has_side_effects=True, vmem_limit_bytes=48 * 2**20
         ),
         name="exchange",
-    )(
-        blk_u, blk_v, prow_u, prow_v, pcol_u, pcol_v, linv, omega, child_u, child_v, child_dest,
-        child_block,
-    )
+    )(*(pltpu.with_memory_space_constraint(a, pltpu.HBM) for a in arguments))
     return pl.pallas_call(
         finish_kernel,
         out_shape=(
@@ -467,20 +509,24 @@
             jax.ShapeDtypeStruct(prow_v.shape, HALF),
             jax.ShapeDtypeStruct(pcol_v.shape, HALF),
         ),
-        in_specs=[anywhere, anywhere, scalars, anywhere, anywhere],
+        in_specs=[inside, inside, scalars, anywhere, anywhere],
         out_specs=(anywhere,) * 3,
         scratch_shapes=[
             half(*blk_u.shape),
-            half(2 * COLS, rank, order),
             pltpu.SMEM((rows * cols,), jnp.int32),
             pltpu.SMEM((2 * COLS,), jnp.int32),
             dma((rows,)),
-            dma((rows,)),
-            dma((3,)),
+            dma((2,)),
         ],
-        compiler_params=pltpu.CompilerParams(vmem_limit_bytes=32 * 2**20),
+        compiler_params=pltpu.CompilerParams(vmem_limit_bytes=24 * 2**20),
         name="finish",
-    )(partial, received.reshape(2 * COLS, rank, order), labels, row_solved, col_solved)
+    )(
+        pltpu.with_memory_space_constraint(partial, pltpu.VMEM),
+        pltpu.with_memory_space_constraint(received, pltpu.VMEM),
+        pltpu.with_memory_space_constraint(labels, pltpu.VMEM),
+        pltpu.with_memory_space_constraint(row_solved, pltpu.VMEM),
+        pltpu.with_memory_space_constraint(col_solved, pltpu.VMEM),
+    )
 
 
 def solution(mesh):

time: 90.6 us -> 67.5 us (0.75)
  the two profiles are of different devices: /device:TPU:14 before, /device:TPU:4 now
where the time goes in v2:
time: 67.5 us; the launch traced here: 67.4 us
  Pallas kernels  66.8 us (99%)
    pallas_call x1, Pallas kernels, body(): pl.pallas_call(exchange_kernel, out_shape=(pltpu.VMEM(blk_u.shape, HALF),...  61.7 us
    pallas_call x1, Pallas kernels, body(): pl.pallas_call(finish_kernel, out_shape=(jax.ShapeDtypeStruct(blk_u.shape...  5.11 us

profile of v2, /device:TPU:4, one launch (start us, length us, event | category | flops | bytes accessed | tf_op | source)
XLA Modules:
  0.0 67.4 jit_solution(6495403707724778355)
XLA Ops:
  0.6 61.7 %exchange.1 = (bf16[12,8,64,512]{3,2,1,0:T(8,128)(2,1)S(1)}, bf16[16,128,512]{2,1,0:T(8,128)(2,1)S(1)}, s32[16,8,128]{2,1,0:T(8,128)S(1)}, bf16[6,64,512]{2,1,0:T(8,128)(2,1)S(1)}, bf16[16,64,512]{2,1,0:T(8,128)(2,1)S(1)}) custom-call(bf16[12,8,64,512]{3,2,1,0:T(8,128)(2,1)} %blk_u.1, bf16[12,8,64,512]{3,2,1,0:T(8,128)(2,1)} %blk_v.1, ...), custom_call_target="tpu_custom_call" | custom-call | tf_op jit(solution)/shard_map/exchange/pallas_call | solution.py:452
  62.3 5.1 %finish.1 = (bf16[12,8,64,512]{3,2,1,0:T(8,128)(2,1)}, bf16[6,64,512]{2,1,0:T(8,128)(2,1)}, bf16[16,64,512]{2,1,0:T(8,128)(2,1)}) custom-call(bf16[12,8,64,512]{3,2,1,0:T(8,128)(2,1)S(1)} %get-tuple-element.8.partial, bf16[16,128,512]{2,1,0:T(8,128)(2,1)S(1)} %get-tuple-element.9.rcv, s32[16,8,128]{2,1,0:T(8,128)S(1)} %get-tuple-element.10.lab, ...), custom_call_target="tpu_custom_call" | custom-call | tf_op jit(solution)/shard_map/finish/pallas_call | solution.py:505

commit v3 on v2

--- a/solution.py
+++ b/solution.py
@@ -42,8 +42,8 @@
 def exchange_kernel(
     blk_u, blk_v, prow_u, prow_v, pcol_u, pcol_v, linv, omega, child_u, child_v, child_dest, child_block,
     t_out, rcv, lab, prow_l, pcol_l,
-    cu, cv, om, snd, lsnd, lin, pu, pv, bu, bv, pcu, pcv, pcl, pvo, prl, gt,
-    vq, cdest, cblock, local, chs, chr_, las, lar, lis, lir, sib, us, ur, vs, vr, gs, gr, bsem, tsem,
+    cu, cv, om, snd, lsnd, lin, pu, pv, bu, bv, acc, pcu, pcv, pvo, et, gt,
+    vq, cdest, cblock, local, chs, chr_, las, lar, lis, lir, sib, us, ur, vs, vr, gs, gr, bsem,
 ):
     row, col = lax.axis_index("row"), lax.axis_index("col")
     x, z = col // SIDE, col % SIDE
@@ -77,7 +77,12 @@
         pltpu.make_async_copy(child_dest, cdest, local.at[9]),
         pltpu.make_async_copy(child_block, cblock, local.at[10]),
     ]
-    for copy in scalar_copies + first:
+    second = [
+        pltpu.make_async_copy(pcol_u, pcu, local.at[4]),
+        pltpu.make_async_copy(pcol_v, pcv, local.at[5]),
+        pltpu.make_async_copy(prow_v, pvo, local.at[6]),
+    ]
+    for copy in scalar_copies + first + second:
         copy.start()
 
     barrier = pltpu.get_barrier_semaphore()
@@ -109,16 +114,59 @@
             greet(dev(i, x, z, core))
             greet(dev(y, i, z, core))
 
+    for copy in scalar_copies + first[:3]:
+        copy.wait()
+    lane = lax.broadcasted_iota(jnp.int32, lsnd.shape[1:], 1)
+
+    def contribution(o):
+        dx, dz = OFFSETS[o]
+        dest = SIDE * ((x + dx) % SIDE) + (z + dz) % SIDE
+
+        def find(c, found):
+            one, two = found
+            hit = cdest[c] == dest
+            two = jnp.where(hit & (one >= 0), c, two)
+            one = jnp.where(hit & (one < 0), c, one)
+            return one, two
+
+        one, two = lax.fori_loop(0, count, find, (jnp.int32(-1), jnp.int32(-1)), unroll=True)
+        label_one = jnp.where(one >= 0, cblock[jnp.maximum(one, 0)], -1)
+        label_two = jnp.where(two >= 0, cblock[jnp.maximum(two, 0)], -1)
+        one, two = jnp.maximum(one, 0), jnp.maximum(two, 0)
+        lsnd[o] = jnp.where(lane == 0, label_one, label_two)
+        v = jnp.concatenate([cv[one], cv[two]], 0)
+        u = jnp.concatenate([cu[one], cu[two]], 0)
+        snd[o] = sketch_of(om[...], v, u, rank).astype(HALF)
+
+    early = 2
+    for o in range(early):
+        contribution(o)
+
+    for copy in second:
+        copy.wait()
+
+    @pl.when(source)
+    def _():
+        base = cols * (z % 2)
+        for h in range(2):
+            j = base + 4 * h
+            qu = pcu[pl.ds(j, 4)].reshape(4 * rank, order)
+            qv = pcv[pl.ds(j, 4)].reshape(4 * rank, order)
+            et[h] = sketch_of(om[...], qu, qv, rank).astype(HALF)
+
     pl.semaphore_wait(barrier, awaited)
 
-    lin_copies = []
-    for o, (dx, dz) in enumerate(OFFSETS[:-1]):
-        copy = remote(
-            linv.at[pl.ds(half_rows * core, half_rows)], lin.at[col, core],
-            lis.at[o], lir.at[o], dev(x + dx, y, z + dz, core),
-        )
-        copy.start()
-        lin_copies.append(copy)
+    def e_remote(h, dy, to_core, recv):
+        return remote(
+            et.at[h], et.at[h], gs.at[2 * dy + h], gr.at[recv], dev(x, y + dy, z, to_core)
+        )
+
+    @pl.when(source)
+    def _():
+        for h in range(2):
+            for dy in (1, 3, 2):
+                e_remote(h, dy, h, 0).start()
+            e_remote(h, 0, 1 - core, (core + h + 1) % 2).start()
 
     place = pl.ds(held * (z % 2), held)
     fourth = rank // SIDE
@@ -163,6 +211,24 @@
             pltpu.make_async_copy(
                 prow_u.at[:, quarter], pu.at[place, quarter], ur.at[y]
             ).start()
+
+    lin_copies = []
+    for o, (dx, dz) in enumerate(OFFSETS[:-1]):
+        copy = remote(
+            linv.at[pl.ds(half_rows * core, half_rows)], lin.at[col, core],
+            lis.at[o], lir.at[o], dev(x + dx, y, z + dz, core),
+        )
+        copy.start()
+        lin_copies.append(copy)
+
+    def pass_e():
+        @pl.when(jnp.logical_not(source))
+        def _():
+            remote(et.at[core], et.at[core], gs.at[0], gr.at[0], sibling).wait_recv()
+
+        @pl.when(y != x)
+        def _():
+            remote(et.at[core], et.at[core], gs.at[0], gr.at[1], sibling).start()
 
     def pass_v():
         for e in range(2):
@@ -186,32 +252,14 @@
             for dz in (1, 3, 2):
                 u_second(dz).start()
 
-    for copy in scalar_copies + first[:3]:
-        copy.wait()
-    lane = lax.broadcasted_iota(jnp.int32, lsnd.shape[1:], 1)
     child_copies = []
     for o, (dx, dz) in enumerate(OFFSETS):
+        if o == 10:
+            pass_v()
         if o == 2:
-            pass_v()
-        if o == 4:
             pass_u()
-        dest = SIDE * ((x + dx) % SIDE) + (z + dz) % SIDE
-
-        def find(c, found, dest=dest):
-            one, two = found
-            hit = cdest[c] == dest
-            two = jnp.where(hit & (one >= 0), c, two)
-            one = jnp.where(hit & (one < 0), c, one)
-            return one, two
-
-        one, two = lax.fori_loop(0, count, find, (jnp.int32(-1), jnp.int32(-1)))
-        label_one = jnp.where(one >= 0, cblock[jnp.maximum(one, 0)], -1)
-        label_two = jnp.where(two >= 0, cblock[jnp.maximum(two, 0)], -1)
-        one, two = jnp.maximum(one, 0), jnp.maximum(two, 0)
-        lsnd[o] = jnp.where(lane == 0, label_one, label_two)
-        v = jnp.concatenate([cv[one], cv[two]], 0)
-        u = jnp.concatenate([cu[one], cu[two]], 0)
-        snd[o] = sketch_of(om[...], v, u, rank).astype(HALF)
+        if o >= early:
+            contribution(o)
         if (dx, dz) == (0, 0):
             copies = [
                 pltpu.make_async_copy(snd.at[o], rcv.at[col], chs.at[o]),
@@ -227,14 +275,6 @@
             copy.start()
         child_copies += copies
 
-    second = [
-        pltpu.make_async_copy(pcol_v, pcv, local.at[4]),
-        pltpu.make_async_copy(prow_v, pvo, local.at[5]),
-        pltpu.make_async_copy(pcol_u, pcu, local.at[6]),
-    ]
-    for copy in second:
-        copy.start()
-
     def block_copies(i):
         return (
             pltpu.make_async_copy(blk_u.at[i], bu.at[i], bsem.at[0, i]),
@@ -244,57 +284,41 @@
     for i in range(rows):
         for copy in block_copies(i):
             copy.start()
+
+    pass_e()
 
     first[3].wait()
     for copy in lin_copies:
         copy.wait_recv()
     share = remote(lin.at[:, core], lin.at[:, core], sib.at[0], sib.at[1], sibling)
     share.start()
+
+    def base_row(i, carry):
+        for copy in block_copies(i):
+            copy.wait()
+        for h in range(2):
+            v = bv[i, 4 * h : 4 * h + 4].reshape(4 * rank, order)
+            u = bu[i, 4 * h : 4 * h + 4].reshape(4 * rank, order)
+            acc[i, h] = sketch_of(om[...], v, u, rank)
+        return carry
+
+    lax.fori_loop(0, rows, base_row, 0)
+
     share.wait_recv()
-
     inverse = lin[...].reshape(order, order)
-    for copy in second:
-        copy.wait()
     piece = 4
     for j in range(0, pcol_v.shape[0], piece):
         part = pcv[j : j + piece].reshape(piece * rank, order)
-        pcl[j : j + piece] = nt(part, inverse).astype(HALF).reshape(piece, rank, order)
-    prl[...] = nt(pvo[...].reshape(held * rank, order), inverse).astype(HALF).reshape(prl.shape)
-    solved = [
-        pltpu.make_async_copy(pcl, pcol_l, local.at[7]),
-        pltpu.make_async_copy(prl, prow_l, local.at[8]),
-    ]
-    for copy in solved:
-        copy.start()
-
-    def g_remote(h, dy, dc_core, recv):
-        return remote(
-            gt.at[h], gt.at[h], gs.at[2 * dy + h], gr.at[recv], dev(x, y + dy, z, dc_core)
-        )
-
-    @pl.when(source)
-    def _():
-        base = cols * (z % 2)
-        for h in range(2):
-            j = base + 4 * h
-            qu = pcu[pl.ds(j, 4)].reshape(4 * rank, order)
-            cl = pcl[pl.ds(j, 4)].reshape(4 * rank, order)
-            gt[h] = sketch_of(om[...], qu, cl, rank).astype(HALF)
-            for dy in (1, 3, 2):
-                g_remote(h, dy, h, 0).start()
-            g_remote(h, 0, 1 - core, (core + h + 1) % 2).start()
+        pcol_l[j : j + piece] = nt(part, inverse).astype(HALF).reshape(piece, rank, order)
+    prow_l[...] = nt(pvo[...].reshape(held * rank, order), inverse).astype(HALF).reshape(
+        prow_l.shape
+    )
 
     @pl.when(jnp.logical_not(source))
     def _():
-        remote(gt.at[core], gt.at[core], gs.at[0], gr.at[0], sibling).wait_recv()
-
-    @pl.when(y != x)
-    def _():
-        remote(gt.at[core], gt.at[core], gs.at[0], gr.at[1], sibling).start()
-
-    @pl.when(jnp.logical_not(source))
-    def _():
-        remote(gt.at[1 - core], gt.at[1 - core], gs.at[0], gr.at[1], sibling).wait_recv()
+        remote(et.at[1 - core], et.at[1 - core], gs.at[0], gr.at[1], sibling).wait_recv()
+
+    gt[...] = nt(et[...].reshape(gt.shape), inverse).astype(HALF)
 
     for e in range(2):
         mine = pu.at[pl.ds(held * e, held)]
@@ -313,27 +337,19 @@
         near_v = pv[pl.ds(2 * ii, 2)].reshape(2 * rank, order)
         near_u = pu[pl.ds(2 * ii, 2)].reshape(2 * rank, order)
         near_l = nt(near_v, lin[...].reshape(order, order)).astype(HALF)
-        coupled = nt(gt[...].reshape(cols * rank, order), near_l).astype(HALF)
+        coupled = nt(gt[...], near_l).astype(HALF)
         for b in range(2):
             i = 2 * ii + b
-            for copy in block_copies(i):
-                copy.wait()
             mine = jnp.where(lanes // rank == b, coupled, jnp.zeros_like(coupled))
             for h in range(2):
-                v = bv[i, 4 * h : 4 * h + 4].reshape(4 * rank, order)
-                u = bu[i, 4 * h : 4 * h + 4].reshape(4 * rank, order)
-                part = sketch_of(om[...], v, u, rank)
-                part = part - nn(mine[4 * rank * h : 4 * rank * (h + 1)], near_u)
-                bv[i, 4 * h : 4 * h + 4] = part.astype(HALF).reshape(4, rank, order)
-            pltpu.make_async_copy(bv.at[i], t_out.at[i], tsem.at[i]).start()
+                update = nn(mine[4 * rank * h : 4 * rank * (h + 1)], near_u)
+                t_out[i, 4 * h : 4 * h + 4] = (
+                    (acc[i, h] - update).astype(HALF).reshape(4, rank, order)
+                )
         return carry
 
     lax.fori_loop(0, rows // 2, pair, 0)
 
-    for i in range(rows):
-        pltpu.make_async_copy(bv.at[i], t_out.at[i], tsem.at[i]).wait()
-    for copy in solved:
-        copy.wait()
     for copy in lin_copies:
         copy.wait_send()
     share.wait_send()
@@ -342,12 +358,12 @@
     def _():
         for h in range(2):
             for dy in (1, 3, 2):
-                g_remote(h, dy, h, 0).wait_send()
-            g_remote(h, 0, 1 - core, 0).wait_send()
+                e_remote(h, dy, h, 0).wait_send()
+            e_remote(h, 0, 1 - core, 0).wait_send()
 
     @pl.when(y != x)
     def _():
-        remote(gt.at[core], gt.at[core], gs.at[0], gr.at[1], sibling).wait_send()
+        remote(et.at[core], et.at[core], gs.at[0], gr.at[1], sibling).wait_send()
 
     @pl.when(keeper)
     def _():
@@ -454,29 +470,29 @@
         out_shape=(
             pltpu.VMEM(blk_u.shape, HALF),
             pltpu.VMEM((COLS, 2 * rank, order), HALF),
-            pltpu.VMEM((COLS, 8, 128), jnp.int32),
+            pltpu.VMEM((COLS, 1, 128), jnp.int32),
             pltpu.VMEM(prow_v.shape, HALF),
             pltpu.VMEM(pcol_v.shape, HALF),
         ),
         in_specs=[anywhere] * 12,
-        out_specs=(anywhere,) * 5,
+        out_specs=(inside, anywhere, anywhere, inside, inside),
         scratch_shapes=[
             half(count, rank, order),
             half(count, rank, order),
             half(rank, order),
             half(COLS, 2 * rank, order),
-            pltpu.VMEM((COLS, 8, 128), jnp.int32),
+            pltpu.VMEM((COLS, 1, 128), jnp.int32),
             half(COLS, 2, linv.shape[0] // 2, order),
             half(rows, rank, order),
             half(rows, rank, order),
             half(*blk_u.shape),
             half(*blk_v.shape),
-            half(held_cols, rank, order),
+            pltpu.VMEM((rows, 2, cols * rank // 2, order), FULL),
             half(held_cols, rank, order),
             half(held_cols, rank, order),
             half(held, rank, order),
-            half(held, rank, order),
             half(2, cols * rank // 2, order),
+            half(cols * rank, order),
             half(rows, rank // SIDE, order),
             pltpu.SMEM(child_block.shape, jnp.int32),
             pltpu.SMEM(child_block.shape, jnp.int32),
@@ -495,7 +511,6 @@
             dma((8,)),
             dma((2,)),
             dma((2, rows)),
-            dma((rows,)),
         ],
         compiler_params=pltpu.CompilerParams(
             collective_id=0, has_side_effects=True, vmem_limit_bytes=48 * 2**20

time: 67.5 us -> 54.6 us (0.81)
  the two profiles are of different devices: /device:TPU:4 before, /device:TPU:1 now
where the time goes in v3:
time: 54.6 us; the launch traced here: 54.4 us
  Pallas kernels  53.8 us (99%)
  between operations  0.64 us (1%)
    pallas_call x1, Pallas kernels, body(): pl.pallas_call(exchange_kernel, out_shape=(pltpu.VMEM(blk_u.shape, HALF),...  49.5 us
    pallas_call x1, Pallas kernels, body(): pl.pallas_call(finish_kernel, out_shape=(jax.ShapeDtypeStruct(blk_u.shape...  4.29 us

profile of v3, /device:TPU:1, one launch (start us, length us, event | category | flops | bytes accessed | tf_op | source)
XLA Modules:
  0.0 54.4 jit_solution(3170438245743636678)
XLA Ops:
  0.6 49.5 %exchange.1 = (bf16[12,8,64,512]{3,2,1,0:T(8,128)(2,1)S(1)}, bf16[16,128,512]{2,1,0:T(8,128)(2,1)S(1)}, s32[16,1,128]{2,1,0:T(1,128)S(1)}, bf16[6,64,512]{2,1,0:T(8,128)(2,1)S(1)}, bf16[16,64,512]{2,1,0:T(8,128)(2,1)S(1)}) custom-call(bf16[12,8,64,512]{3,2,1,0:T(8,128)(2,1)} %blk_u.1, bf16[12,8,64,512]{3,2,1,0:T(8,128)(2,1)} %blk_v.1, ...), custom_call_target="tpu_custom_call" | custom-call | tf_op jit(solution)/shard_map/exchange/pallas_call | solution.py:468
  50.1 4.3 %finish.1 = (bf16[12,8,64,512]{3,2,1,0:T(8,128)(2,1)}, bf16[6,64,512]{2,1,0:T(8,128)(2,1)}, bf16[16,64,512]{2,1,0:T(8,128)(2,1)}) custom-call(bf16[12,8,64,512]{3,2,1,0:T(8,128)(2,1)S(1)} %get-tuple-element.8.partial, bf16[16,128,512]{2,1,0:T(8,128)(2,1)S(1)} %get-tuple-element.9.rcv, s32[16,1,128]{2,1,0:T(1,128)S(1)} %get-tuple-element.10.lab, ...), custom_call_target="tpu_custom_call" | custom-call | tf_op jit(solution)/shard_map/finish/pallas_call | solution.py:520

commit v4 on v3

--- a/solution.py
+++ b/solution.py
@@ -64,6 +64,8 @@
             src_ref=src, dst_ref=dst, send_sem=send, recv_sem=recv, device_id=to,
             device_id_type=MESH,
         )
+
+    lin[...] = jnp.zeros_like(lin)
 
     first = [
         pltpu.make_async_copy(child_v, cv, local.at[0]),
@@ -212,14 +214,19 @@
                 prow_u.at[:, quarter], pu.at[place, quarter], ur.at[y]
             ).start()
 
-    lin_copies = []
-    for o, (dx, dz) in enumerate(OFFSETS[:-1]):
-        copy = remote(
-            linv.at[pl.ds(half_rows * core, half_rows)], lin.at[col, core],
+    def lin_copy(o, n):
+        dx, dz = OFFSETS[o]
+        tiles = pl.ds(0, order // SIDE * (n + 1))
+        return remote(
+            linv.at[pl.ds(half_rows * core, half_rows), tiles], lin.at[col, core, :, tiles],
             lis.at[o], lir.at[o], dev(x + dx, y, z + dz, core),
         )
-        copy.start()
-        lin_copies.append(copy)
+
+    for n in range(SIDE):
+        @pl.when(x == n)
+        def _():
+            for o in range(COLS - 1):
+                lin_copy(o, n).start()
 
     def pass_e():
         @pl.when(jnp.logical_not(source))
@@ -288,8 +295,14 @@
     pass_e()
 
     first[3].wait()
-    for copy in lin_copies:
-        copy.wait_recv()
+    for n in range(SIDE):
+        for turn in range(SIDE):
+            @pl.when((x + SIDE - turn) % SIDE == n)
+            def _():
+                for o in range(COLS - 1):
+                    if OFFSETS[o][0] == turn:
+                        lin_copy(o, n).wait_recv()
+
     share = remote(lin.at[:, core], lin.at[:, core], sib.at[0], sib.at[1], sibling)
     share.start()
 
@@ -350,8 +363,12 @@
 
     lax.fori_loop(0, rows // 2, pair, 0)
 
-    for copy in lin_copies:
-        copy.wait_send()
+    for n in range(SIDE):
+        @pl.when(x == n)
+        def _():
+            for o in range(COLS - 1):
+                lin_copy(o, n).wait_send()
+
     share.wait_send()
 
     @pl.when(source)

time: 54.6 us -> 54.3 us (level)
  no operation moved by 1% of the time
where the time goes in v4:
time: 54.3 us; the launch traced here: 54.1 us
  Pallas kernels  53.5 us (99%)
  between operations  0.64 us (1%)
    pallas_call x1, Pallas kernels, body(): pl.pallas_call(exchange_kernel, out_shape=(pltpu.VMEM(blk_u.shape, HALF),...  49.3 us
    pallas_call x1, Pallas kernels, body(): pl.pallas_call(finish_kernel, out_shape=(jax.ShapeDtypeStruct(blk_u.shape...  4.16 us

profile of v4, /device:TPU:1, one launch (start us, length us, event | category | flops | bytes accessed | tf_op | source)
XLA Modules:
  0.0 54.1 jit_solution(11013947826017879906)
XLA Ops:
  0.6 49.3 %exchange.1 = (bf16[12,8,64,512]{3,2,1,0:T(8,128)(2,1)S(1)}, bf16[16,128,512]{2,1,0:T(8,128)(2,1)S(1)}, s32[16,1,128]{2,1,0:T(1,128)S(1)}, bf16[6,64,512]{2,1,0:T(8,128)(2,1)S(1)}, bf16[16,64,512]{2,1,0:T(8,128)(2,1)S(1)}) custom-call(bf16[12,8,64,512]{3,2,1,0:T(8,128)(2,1)} %blk_u.1, bf16[12,8,64,512]{3,2,1,0:T(8,128)(2,1)} %blk_v.1, ...), custom_call_target="tpu_custom_call" | custom-call | tf_op jit(solution)/shard_map/exchange/pallas_call | solution.py:485
  50.0 4.2 %finish.1 = (bf16[12,8,64,512]{3,2,1,0:T(8,128)(2,1)}, bf16[6,64,512]{2,1,0:T(8,128)(2,1)}, bf16[16,64,512]{2,1,0:T(8,128)(2,1)}) custom-call(bf16[12,8,64,512]{3,2,1,0:T(8,128)(2,1)S(1)} %get-tuple-element.8.partial, bf16[16,128,512]{2,1,0:T(8,128)(2,1)S(1)} %get-tuple-element.9.rcv, s32[16,1,128]{2,1,0:T(1,128)S(1)} %get-tuple-element.10.lab, ...), custom_call_target="tpu_custom_call" | custom-call | tf_op jit(solution)/shard_map/finish/pallas_call | solution.py:537
